TPU v7x, 32 devices: a whole 2x2x4 slice. The times are simulated.
32 devices in a mesh: tiles: 8 (over z, x), pair: 4 (over y, core).
Axes of the slice: x: 2, y: 2, z: 4, core: 2. Of those that a mesh axis runs over, the one named last changes fastest.
Arguments:
- t2: bfloat16 [256, 16, 4096], P('tiles', None, 'pair'), may hold values from -6 to 6
- v_plus: bfloat16 [8, 64, 16, 2048], P('tiles'), may hold values from -0.1875 to 0.1875
- v_minus: bfloat16 [8, 64, 16, 2048], P('tiles'), may hold values from -0.1875 to 0.1875
- partner: int32 [4096], P('pair'), may hold values from 0 to 1023, as said below
- win_tile: int32 [8, 64], replicated, may hold values from 0 to 255, as said below
- win_count: int32 [8], replicated, may hold values from 48 to 64, as said below
Outputs:
- ladder: bfloat16 [4096, 16384], P('pair', 'tiles')
Inputs may be any that keep to these rules, and one draw needn't show every extreme that they name: `partner`: each block of 1024 entries is a permutation of 0 to 1023, and blocks 2h and 2h + 1 are inverse to each other. `win_tile`: the live entries of one owner's list name distinct tiles; at most 8 of them lie among one index of tiles' 32 tiles (tiles k * 32 to (k + 1) * 32 - 1), and some owner takes exactly 8 from one index in every draw. Entries past the live count name tiles too. `win_count`: some owner has exactly 64 live slots.
All inputs are finite; a program needn't handle non-finite values.
Results may differ from a plain program's by a relative error of at most 0.0052.
Values may be sent and summed in bfloat16 or wider, within the bound.
A program may use at most 128 MiB of HBM per device.

v0:
```python
import jax
import jax.numpy as jnp
from jax import lax
from jax.sharding import PartitionSpec as P


def partner_2(x, axis, stride):
    return lax.ppermute(x, axis, [(i, i ^ 1 << stride) for i in range(lax.axis_size(axis))])


def route_plan(win_tile, win_count, per_source):
    window_slots = win_tile.shape[1]
    sources = win_tile // per_source
    offsets = win_tile % per_source
    positions = jnp.arange(window_slots)
    living = positions[None, :] < win_count[:, None]
    earlier = positions[None, None, :] < positions[None, :, None]
    same_source = (sources[:, :, None] == sources[:, None, :]) & living[:, None, :] & earlier
    ranked = jnp.sum(same_source, axis=2)
    return (sources, offsets, ranked, living)


def pack_sends(payload, sources, offsets, ranked, living, owner_index, capacity):
    per_source = payload.shape[0]
    owner_count = sources.shape[0]
    hits = (living & (sources == owner_index)).astype(jnp.float32)
    rank_hot = (ranked[:, :, None] == jnp.arange(capacity)[None, None, :]).astype(jnp.float32)
    tile_hot = (offsets[:, :, None] == jnp.arange(per_source)[None, None, :]).astype(jnp.float32)
    select = jnp.einsum("ow,owc,owt->oct", hits, rank_hot, tile_hot).astype(jnp.bfloat16)
    select = select.reshape(owner_count * capacity, per_source)
    outgoing = jnp.dot(select, payload, preferred_element_type=jnp.float32).astype(jnp.bfloat16)
    return outgoing.reshape(owner_count, capacity, payload.shape[1])


def unpack_window(received, source_row, rank_row, living_row, capacity):
    owner_count = received.shape[0]
    flat = received.reshape(owner_count * capacity, received.shape[2])
    target = source_row * capacity + rank_row
    picking = living_row[:, None] & (target[:, None] == jnp.arange(owner_count * capacity)[None, :])
    return jnp.dot(picking.astype(jnp.bfloat16), flat, preferred_element_type=jnp.float32).astype(
        jnp.bfloat16
    )


def body(t2, v_plus, v_minus, partner, win_tile, win_count):
    per_source, tile_width, pair_rows = t2.shape
    owner_count = lax.axis_size("tiles")
    window_slots = win_tile.shape[1]
    capacity = max(2, (window_slots + owner_count - 1) // owner_count)
    owner_index = lax.axis_index("tiles")
    sources, offsets, ranked, living = route_plan(win_tile, win_count, per_source)
    source_row = lax.dynamic_index_in_dim(sources, owner_index, 0, keepdims=False)
    rank_row = lax.dynamic_index_in_dim(ranked, owner_index, 0, keepdims=False)
    living_row = lax.dynamic_index_in_dim(living, owner_index, 0, keepdims=False)
    plus_slab = v_plus[0]
    minus_slab = v_minus[0]
    outgoing = pack_sends(
        t2.reshape(per_source, tile_width * pair_rows),
        sources,
        offsets,
        ranked,
        living,
        owner_index,
        capacity,
    )
    received = lax.all_to_all(outgoing, "tiles", split_axis=0, concat_axis=0, tiled=True)
    own_window = unpack_window(received, source_row, rank_row, living_row, capacity).reshape(
        window_slots, tile_width, pair_rows
    )
    mirrored = partner_2(own_window, "pair", 0)
    own_values = own_window.astype(jnp.float32)
    mirror_values = jnp.take(mirrored, partner, axis=2).astype(jnp.float32)
    wplus = (own_values + mirror_values).astype(jnp.bfloat16)
    wminus = (own_values - mirror_values).astype(jnp.bfloat16)
    contract = (((0, 1), (0, 1)), ((), ()))
    summed = lax.dot_general(wplus, plus_slab, contract, preferred_element_type=jnp.float32)
    summed = summed + lax.dot_general(
        wminus, minus_slab, contract, preferred_element_type=jnp.float32
    )
    ladder = (0.5 * summed).astype(jnp.bfloat16)
    return ladder


def solution(mesh):
    placed = (
        P("tiles", None, "pair"),
        P("tiles", None, None, None),
        P("tiles", None, None, None),
        P("pair"),
        P(),
        P(),
    )
    return jax.shard_map(
        body, mesh=mesh, in_specs=placed, out_specs=P("pair", "tiles"), check_vma=False
    )
```

profile of v0, /device:TPU:1, one launch (start us, length us, event | category | flops | bytes accessed | tf_op | source)
XLA Modules:
  0.0 111.9 jit_solution(14147903340394442369)
XLA Ops:
  0.0 0.7 add_select_fusion.1
  0.8 1.8 %copy.21 = bf16[4,8,16,1024]{3,1,2,0:T(8,128)(2,1)S(1)} copy(bf16[4,8,16,1024]{3,2,1,0:T(8,128)(2,1)} %bitcast.54) | data formatting | bytes 2097152
  2.6 0.1 iota_compare_fusion.8
  2.7 0.3 convert_reduce_fusion
  3.0 2.1 %fusion = bf16[8,8,16384]{2,1,0:T(8,128)(2,1)} fusion(bf16[32,16384]{1,0:T(8,128)(2,1)S(1)} %bitcast.50, s32[8,64]{1,0:T(8,128)S(1)} %get-tuple-element.8, bf16[8,64]{1,0:T(8,128)(2,1)S(1)} %get-tuple-element.10, s32[8,64]{1,0:T(8,128)S(1)} %convert_reduce_fusion), kind=kOutput, calls=%fused_computation.3 | convolution fusion | flops 68444160 | bytes 3150848 | tf_op jit(solution)/shard_map/dot_general | solution.py:31
  5.1 6.4 %all-to-all-start = ((bf16[8,8,16384]{2,1,0:T(8,128)(2,1)}), bf16[8,8,16384]{2,1,0:T(8,128)(2,1)}, u32[]{:S(2)}, u32[]{:S(2)}) async-start(bf16[8,8,16384]{2,1,0:T(8,128)(2,1)} %fusion), calls=%async_computation | async-start | bytes 4194304 | tf_op jit(solution)/shard_map/all_to_all | solution.py:66
  11.5 47.4 %all-to-all-done = bf16[8,8,16384]{2,1,0:T(8,128)(2,1)} async-done(((bf16[8,8,16384]{2,1,0:T(8,128)(2,1)}), bf16[8,8,16384]{2,1,0:T(8,128)(2,1)}, u32[]{:S(2)}, u32[]{:S(2)}) %all-to-all-start) | async-done | bytes 2097184 | tf_op jit(solution)/shard_map/all_to_all | solution.py:66
  59.0 2.3 %convolution_convert_fusion = bf16[64,16384]{1,0:T(8,128)(2,1)S(1)} fusion(bf16[8,8,16384]{2,1,0:T(8,128)(2,1)} %all-to-all-done, s32[64]{0:T(128)S(1)} %fusion.29, pred[64]{0:T(512)(128)(4,1)S(1)} %dynamic-slice_bitcast_fusion), kind=kOutput, calls=%fused_computation.1 | convolution fusion | flops 135274496 | bytes 4194624 | tf_op jit(solution)/shard_map/dot_general | solution.py:40
  61.3 0.0 copy-start.1
  61.3 1.2 %copy.23 = bf16[8,8,16,1024]{3,2,1,0:T(8,128)(2,1)S(1)} copy(bf16[8,8,16,1024]{3,1,2,0:T(8,128)(2,1)S(1)} %bitcast.44) | data formatting | bytes 4194304
  62.6 1.9 %collective-permute-start = (bf16[64,16,1024]{2,1,0:T(8,128)(2,1)S(1)}, bf16[64,16,1024]{2,1,0:T(8,128)(2,1)}, u32[]{:S(2)}, u32[]{:S(2)}) collective-permute-start(bf16[64,16,1024]{2,1,0:T(8,128)(2,1)S(1)} %bitcast.51), channel_id=1, source_target_pairs={{0,1},{1,0},{2,3},{3,2},{4,5},{5,4},{6,7},{7,6},{8,9},{9,8},{10,11... | collective-permute-start | bytes 6291464 | tf_op jit(solution)/shard_map/ppermute | solution.py:8
  64.5 3.9 %collective-permute-done = bf16[64,16,1024]{2,1,0:T(8,128)(2,1)} collective-permute-done((bf16[64,16,1024]{2,1,0:T(8,128)(2,1)S(1)}, bf16[64,16,1024]{2,1,0:T(8,128)(2,1)}, u32[]{:S(2)}, u32[]{:S(2)}) %collective-permute-start) | collective-permute-done | bytes 2097184 | tf_op jit(solution)/shard_map/ppermute | solution.py:8
  68.4 8.2 %copy.19 = bf16[64,16,1024]{0,1,2:T(8,128)(2,1)} copy(bf16[64,16,1024]{2,1,0:T(8,128)(2,1)} %collective-permute-done) | data formatting | bytes 4194304 | tf_op jit(solution)/shard_map/ppermute | solution.py:8
  76.5 10.5 %gather_fusion = bf16[1024,64,16]{1,2,0:T(8,128)(2,1)} fusion(bf16[64,16,1024]{0,1,2:T(8,128)(2,1)} %copy.19, s32[1024]{0:T(1024)S(1)} %fusion.25), kind=kCustom, calls=%fused_computation | custom fusion | bytes 4198400 | tf_op jit(solution)/shard_map/jit(_take)/gather | solution.py:72
  87.1 6.8 %copy.20 = bf16[64,16,1024]{2,1,0:T(8,128)(2,1)} copy(bf16[64,16,1024]{0,1,2:T(8,128)(2,1)} %bitcast.45) | data formatting | bytes 4194304 | tf_op jit(solution)/shard_map/jit(_take)/gather | solution.py:72
  93.9 2.8 %copy.24 = bf16[8,8,16,1024]{3,1,2,0:T(8,128)(2,1)S(1)} copy(bf16[8,8,16,1024]{3,2,1,0:T(8,128)(2,1)} %bitcast.46) | data formatting | bytes 4194304
  96.7 1.0 fusion.4
  97.7 1.2 %copy.26 = bf16[8,8,16,1024]{3,2,1,0:T(8,128)(2,1)S(1)} copy(bf16[8,8,16,1024]{3,1,2,0:T(8,128)(2,1)S(1)} %bitcast.49) | data formatting | bytes 4194304
  98.9 0.0 copy-start.3
  98.9 1.2 %copy.25 = bf16[8,8,16,1024]{3,2,1,0:T(8,128)(2,1)S(1)} copy(bf16[8,8,16,1024]{3,1,2,0:T(8,128)(2,1)S(1)} %bitcast.47) | data formatting | bytes 4194304
  100.1 1.0 copy-done.3
  101.1 4.7 %fusion.6 = f32[1024,2048,1]{1,0,2:T(8,128)S(1)} fusion(bf16[64,16,1024]{2,1,0:T(8,128)(2,1)S(1)} %bitcast.53, bf16[1,64,16,2048]{3,2,1,0:T(8,128)(2,1)S(1)} %copy-done.3), kind=kOutput, calls=%fused_computation.12 | convolution fusion | flops 4294967296 | bytes 14680064 | tf_op jit(solution)/shard_map/dot_general | solution.py:76
  105.8 0.0 copy-done.4
  105.8 6.1 %fusion.2 = bf16[1024,2048]{1,0:T(8,128)(2,1)} fusion(f32[1024,2048,1]{1,0,2:T(8,128)S(1)} %fusion.6, bf16[64,16,1024]{2,1,0:T(8,128)(2,1)S(1)} %bitcast.52, bf16[1,64,16,2048]{3,2,1,0:T(8,128)(2,1)S(1)} %copy-done.4), kind=kOutput, calls=%fused_computation.6 | convolution fusion | flops 4301258752 | bytes 18874368 | tf_op jit(solution)/shard_map/dot_general | solution.py:77
  (13 shorter events, 0.1 us)
Async XLA Ops:
  0.0 2.6 %copy-start = (s32[8,64]{1,0:T(8,128)S(1)}, s32[8,64]{1,0:T(8,128)}, u32[]{:S(2)}) copy-start(s32[8,64]{1,0:T(8,128)} %param.10) | copy-start | bytes 6148
  0.0 2.6 %copy-start.2 = (s32[8]{0:T(128)S(1)}, s32[8]{0:T(128)}, u32[]{:S(2)}) copy-start(s32[8]{0:T(128)} %param.11) | copy-start | bytes 100
  5.1 53.8 %all-to-all-start = ((bf16[8,8,16384]{2,1,0:T(8,128)(2,1)}), bf16[8,8,16384]{2,1,0:T(8,128)(2,1)}, u32[]{:S(2)}, u32[]{:S(2)}) async-start(bf16[8,8,16384]{2,1,0:T(8,128)(2,1)} %fusion), calls=%async_computation | async-start | bytes 4194304 | tf_op jit(solution)/shard_map/all_to_all | solution.py:66
  61.3 3.1 %copy-start.1 = (s32[1024]{0:T(1024)S(1)}, s32[1024]{0:T(1024)}, u32[]{:S(2)}) copy-start(s32[1024]{0:T(1024)} %param.9) | copy-start | bytes 12292
  62.6 5.8 %collective-permute-start = (bf16[64,16,1024]{2,1,0:T(8,128)(2,1)S(1)}, bf16[64,16,1024]{2,1,0:T(8,128)(2,1)}, u32[]{:S(2)}, u32[]{:S(2)}) collective-permute-start(bf16[64,16,1024]{2,1,0:T(8,128)(2,1)S(1)} %bitcast.51), channel_id=1, source_target_pairs={{0,1},{1,0},{2,3},{3,2},{4,5},{5,4},{6,7},{7,6},{8,9},{9,8},{10,11... | collective-permute-start | bytes 6291464 | tf_op jit(solution)/shard_map/ppermute | solution.py:8
  98.9 2.2 %copy-start.3 = (bf16[1,64,16,2048]{3,2,1,0:T(8,128)(2,1)S(1)}, bf16[1,64,16,2048]{3,2,1,0:T(8,128)(2,1)}, u32[]{:S(2)}) copy-start(bf16[1,64,16,2048]{3,2,1,0:T(8,128)(2,1)} %param.7) | copy-start | bytes 12582916
  101.1 4.7 %copy-start.4 = (bf16[1,64,16,2048]{3,2,1,0:T(8,128)(2,1)S(1)}, bf16[1,64,16,2048]{3,2,1,0:T(8,128)(2,1)}, u32[]{:S(2)}) copy-start(bf16[1,64,16,2048]{3,2,1,0:T(8,128)(2,1)} %param.8) | copy-start | bytes 12582916
where the time goes:
time: 113 us; the launch traced here: 112 us
  waiting for transfers between devices  51.3 us (45%)
  local copies, waits for them, and re-layouts  34.8 us (31%)
  matrix products  15.3 us (14%)
  starting transfers between devices  8.25 us (7%)
  other arithmetic  2.15 us (2%)
    all_to_all x1, waiting for transfers between devices, body(): lax.all_to_all(outgoing, 'tiles', split_axis=0, concat_axis=0, tiled=True)  47.4 us
    gather x2, local copies, waits for them, and re-layouts, body(): mirror_values = jnp.take(mirrored, partner, axis=2).astype(jnp.float32)  17.4 us
    unnamed x17, local copies, waits for them, and re-layouts  9.24 us
    ppermute x1, local copies, waits for them, and re-layouts, partner_2(): lax.ppermute(x, axis, [(i, i ^ 1 << stride) for i in range(lax.axis_size(...  8.17 us
    all_to_all x1, starting transfers between devices, body(): lax.all_to_all(outgoing, 'tiles', split_axis=0, concat_axis=0, tiled=True)  6.36 us
    dot_general x1, matrix products, body(): lax.dot_general(wminus, minus_slab, contract, preferred_element_type=jnp....  6.13 us
    dot_general x1, matrix products, body(): lax.dot_general(wplus, plus_slab, contract, preferred_element_type=jnp.fl...  4.66 us
    ppermute x1, waiting for transfers between devices, partner_2(): lax.ppermute(x, axis, [(i, i ^ 1 << stride) for i in range(lax.axis_size(...  3.86 us
  transfers between devices with their start and end apart: 2, of which 2 were waited for; matrix products, arithmetic and copies ran while one was open for 0% of the time, Pallas kernels for 0%

commit v1 on v0

v1 whole, which is shorter than its diff:
```python
import functools

import jax
import jax.numpy as jnp
from jax import lax
from jax.experimental import pallas as pl
from jax.experimental.pallas import tpu as pltpu
from jax.sharding import PartitionSpec as P

MESH = pl.DeviceIdType.MESH


def route_plan(win_tile, win_count, per_source, capacity):
    owners, slots = win_tile.shape
    me = lax.axis_index("tiles")
    sources = win_tile // per_source
    offsets = win_tile % per_source
    positions = jnp.arange(slots)
    living = positions[None, :] < win_count[:, None]
    earlier = positions[None, None, :] < positions[None, :, None]
    same = (sources[:, :, None] == sources[:, None, :]) & living[:, None, :] & earlier
    ranked = jnp.sum(same, axis=2, dtype=jnp.int32)
    ranks = jnp.arange(capacity)
    taken = (living & (sources == me))[:, :, None] & (ranked[:, :, None] == ranks)
    send = jnp.sum(jnp.where(taken, offsets[:, :, None], 0), axis=1, dtype=jnp.int32)
    mine = [lax.dynamic_index_in_dim(x, me, 0, keepdims=False) for x in (sources, ranked, living)]
    filled = (
        mine[2][None, None, :]
        & (mine[0][None, None, :] == jnp.arange(owners)[:, None, None])
        & (mine[1][None, None, :] == ranks[None, :, None])
    )
    slot = jnp.sum(jnp.where(filled, positions + 1, 0), axis=2, dtype=jnp.int32) - 1
    return send.reshape(-1), slot.reshape(-1)


def across(me, n, d):
    other, place = 0, 1
    while place < n:
        other = other + ((me // place) % 2 + (d // place) % 2) % 2 * place
        place *= 2
    return other


def kernel(
    n, cap, order,
    send_idx, slot_idx, partner, t2_hbm, vp_hbm, vm_hbm, out_hbm,
    t2, vp, vm, pack, recv, mirror, onehot, vst, wt, acc, staged,
    in_sem, send_sem, recv_sem, fwd_sem, mir_sem, out_sem,
):
    me = lax.axis_index("tiles")
    pair = lax.axis_index("pair")
    sibling = pair + 1 - 2 * (pair % 2)
    tw, rows = t2.shape[1:]
    cols = vp.shape[2]
    depth = cap * tw
    block = 512

    t2_in = pltpu.make_async_copy(t2_hbm, t2, in_sem.at[0])
    t2_in.start()
    vp_in = pltpu.make_async_copy(vp_hbm.at[0], vp, in_sem.at[1])
    vm_in = pltpu.make_async_copy(vm_hbm.at[0], vm, in_sem.at[2])
    vp_in.start()
    vm_in.start()

    barrier = pltpu.get_barrier_semaphore()

    def greet(d, carry):
        pl.semaphore_signal(barrier, inc=1, device_id={"tiles": across(me, n, d)}, device_id_type=MESH)
        return carry

    lax.fori_loop(1, n, greet, 0)
    pl.semaphore_signal(barrier, inc=1, device_id={"pair": sibling}, device_id_type=MESH)
    pl.semaphore_wait(barrier, n)
    t2_in.wait()

    def route(d):
        return pltpu.make_async_remote_copy(
            src_ref=pack.at[d], dst_ref=recv.at[d], send_sem=send_sem.at[d], recv_sem=recv_sem.at[d],
            device_id={"tiles": across(me, n, d)}, device_id_type=MESH,
        )

    def forward(d, src):
        return pltpu.make_async_remote_copy(
            src_ref=src.at[d], dst_ref=mirror.at[d], send_sem=fwd_sem.at[d], recv_sem=mir_sem.at[d],
            device_id={"pair": sibling}, device_id_type=MESH,
        )

    def fill(d):
        owner = across(me, n, d)
        for r in range(cap):
            pack[d, r * tw : (r + 1) * tw] = t2[send_idx[owner * cap + r]]

    def dispatch(d):
        fill(d)
        route(d).start()

    if n <= 8:
        for d in order:
            dispatch(d)
    else:
        lax.fori_loop(1, n, lambda j, c: (dispatch(n - j), c)[1], 0)
    fill(0)
    forward(0, pack).start()

    @pl.loop(0, rows // 128)
    def _(i):
        at = pl.multiple_of(i * 128, 128)
        row = lax.broadcasted_iota(jnp.int32, (128, rows), 0) + at
        onehot[pl.ds(at, 128), :] = (row == partner[...]).astype(jnp.float32).astype(jnp.bfloat16)

    vp_in.wait()
    vm_in.wait()

    def slabs(d):
        source = across(me, n, d)
        for r in range(cap):
            slot = slot_idx[source * cap + r]
            at = jnp.maximum(slot, 0)
            keep = (slot >= 0).astype(jnp.float32).astype(jnp.bfloat16)
            vst[r * tw : (r + 1) * tw, :] = vp[at] * keep
            vst[depth + r * tw : depth + (r + 1) * tw, :] = vm[at] * keep

    def combine(d, src):
        mir = jnp.dot(mirror[d], onehot[...], preferred_element_type=jnp.float32)
        own = src[d].astype(jnp.float32)
        wt[:, :depth] = jnp.transpose(own + mir).astype(jnp.bfloat16)
        wt[:, depth:] = jnp.transpose(own - mir).astype(jnp.bfloat16)

    def product(at):
        return jnp.dot(wt[...], vst[:, pl.ds(at, block)], preferred_element_type=jnp.float32)

    slabs(0)
    forward(0, pack).wait_recv()
    combine(0, pack)

    @pl.loop(0, cols // block)
    def _(i):
        at = pl.multiple_of(i * block, block)
        acc[:, pl.ds(at, block)] = product(at)

    def arrive(d):
        slabs(d)
        route(d).wait_recv()
        forward(d, recv).start()
        forward(d, recv).wait_recv()
        combine(d, recv)

    def add(d):
        arrive(d)

        @pl.loop(0, cols // block)
        def _(i):
            at = pl.multiple_of(i * block, block)
            acc[:, pl.ds(at, block)] += product(at)

    if n <= 8:
        for d in order[:-1]:
            add(d)
        last = order[-1]
    else:
        lax.fori_loop(1, n - 1, lambda j, c: (add(n - j), c)[1], 0)
        last = 1
    arrive(last)
    writes = []
    for i in range(cols // block):
        at = i * block
        staged[:, at : at + block] = (0.5 * (acc[:, at : at + block] + product(at))).astype(jnp.bfloat16)
        write = pltpu.make_async_copy(
            staged.at[:, at : at + block], out_hbm.at[:, at : at + block], out_sem.at[i]
        )
        write.start()
        writes.append(write)

    def settle(d, carry):
        route(d).wait_send()
        forward(d, recv).wait_send()
        return carry

    lax.fori_loop(1, n, settle, 0)
    forward(0, pack).wait_send()
    for write in writes:
        write.wait()


def body(t2, v_plus, v_minus, partner, win_tile, win_count):
    per_source, tw, rows = t2.shape
    n = lax.axis_size("tiles")
    slots, cols = v_plus.shape[1], v_plus.shape[3]
    cap = max(2, (slots + n - 1) // n)
    send, slot = route_plan(win_tile, win_count, per_source, cap)
    order = (7, 1, 6, 2, 5, 3, 4) if n == 8 else tuple(range(n - 1, 0, -1))
    depth = cap * tw
    vmem, smem, hbm = pltpu.VMEM, pltpu.SMEM, pl.ANY
    return pl.pallas_call(
        functools.partial(kernel, n, cap, order),
        out_shape=jax.ShapeDtypeStruct((rows, cols), jnp.bfloat16),
        in_specs=[pl.BlockSpec(memory_space=m) for m in (smem, smem, vmem, hbm, hbm, hbm)],
        out_specs=pl.BlockSpec(memory_space=hbm),
        scratch_shapes=[
            pltpu.VMEM(t2.shape, jnp.bfloat16),
            pltpu.VMEM(v_plus.shape[1:], jnp.bfloat16),
            pltpu.VMEM(v_minus.shape[1:], jnp.bfloat16),
            pltpu.VMEM((n, depth, rows), jnp.bfloat16),
            pltpu.VMEM((n, depth, rows), jnp.bfloat16),
            pltpu.VMEM((n, depth, rows), jnp.bfloat16),
            pltpu.VMEM((rows, rows), jnp.bfloat16),
            pltpu.VMEM((2 * depth, cols), jnp.bfloat16),
            pltpu.VMEM((rows, 2 * depth), jnp.bfloat16),
            pltpu.VMEM((rows, cols), jnp.float32),
            pltpu.VMEM((rows, cols), jnp.bfloat16),
            pltpu.SemaphoreType.DMA((3,)),
            pltpu.SemaphoreType.DMA((n,)),
            pltpu.SemaphoreType.DMA((n,)),
            pltpu.SemaphoreType.DMA((n,)),
            pltpu.SemaphoreType.DMA((n,)),
            pltpu.SemaphoreType.DMA((cols // 512,)),
        ],
        compiler_params=pltpu.CompilerParams(
            collective_id=0, has_side_effects=True, vmem_limit_bytes=56 * 2**20
        ),
        cost_estimate=pl.CostEstimate(
            flops=4 * rows * cols * n * depth, bytes_accessed=16 * 2**20, transcendentals=0
        ),
    )(send, slot, partner.reshape(1, rows), t2, v_plus, v_minus)


def solution(mesh):
    placed = (
        P("tiles", None, "pair"),
        P("tiles", None, None, None),
        P("tiles", None, None, None),
        P("pair"),
        P(),
        P(),
    )
    return jax.shard_map(
        body, mesh=mesh, in_specs=placed, out_specs=P("pair", "tiles"), check_vma=False
    )
```

time: 113 us -> 68.2 us (0.60)
  Pallas kernels: 0 us -> 59.6 us
  waiting for transfers between devices: 51.3 us -> 0 us
  local copies, waits for them, and re-layouts: 34.8 us -> 6.01 us
  matrix products: 15.3 us -> 0 us
  starting transfers between devices: 8.25 us -> 0 us
    pallas_call x0 -> x1, Pallas kernels: none -> 59.6 us  [body(): pl.pallas_call(functools.partial(kernel, n, cap, order), out_shape=jax.Sh...]
    all_to_all x1 -> x0, waiting for transfers between devices: 47.4 us -> none  [body(): lax.all_to_all(outgoing, 'tiles', split_axis=0, concat_axis=0, tiled=True)]
    gather x2 -> x0, local copies, waits for them, and re-layouts: 17.4 us -> none  [body(): mirror_values = jnp.take(mirrored, partner, axis=2).astype(jnp.float32)]
    dot_general x4 -> x0, matrix products: 15.3 us -> none  [the longest x1 6.13 us: body(): lax.dot_general(wminus, minus_slab, contract, preferred_element_type=jnp....]
    ppermute x1 -> x0, local copies, waits for them, and re-layouts: 8.17 us -> none  [partner_2(): lax.ppermute(x, axis, [(i, i ^ 1 << stride) for i in range(lax.axis_size(...]
    all_to_all x1 -> x0, starting transfers between devices: 6.36 us -> none  [body(): lax.all_to_all(outgoing, 'tiles', split_axis=0, concat_axis=0, tiled=True)]
    unnamed x17 -> x1, local copies, waits for them, and re-layouts: 9.24 us -> 4.79 us
    ppermute x1 -> x0, waiting for transfers between devices: 3.86 us -> none  [partner_2(): lax.ppermute(x, axis, [(i, i ^ 1 << stride) for i in range(lax.axis_size(...]
  transfers between devices with their start and end apart: 2 -> 0, of which waited for: 2 -> 0; matrix products, arithmetic and copies ran while one was open for 0% -> 0% of each run, Pallas kernels for 0% -> 0%
where the time goes in v1:
time: 68.2 us; the launch traced here: 68 us
  Pallas kernels  59.6 us (87%)
  local copies, waits for them, and re-layouts  6.01 us (9%)
  other arithmetic  2.25 us (3%)
    pallas_call x1, Pallas kernels, body(): pl.pallas_call(functools.partial(kernel, n, cap, order), out_shape=jax.Sh...  59.6 us
    unnamed x1, local copies, waits for them, and re-layouts  4.79 us

profile of v1, /device:TPU:1, one launch (start us, length us, event | category | flops | bytes accessed | tf_op | source)
XLA Modules:
  0.0 68.0 jit_solution(12161147555392405880)
XLA Ops:
  0.0 0.7 %add_select_fusion = s32[8,64]{1,0:T(8,128)S(1)} fusion(s32[8,64]{1,0:T(8,128)} %param.10), kind=kLoop, calls=%fused_computation.6 | loop fusion | flops 5632 | bytes 4096 | tf_op jit(solution)/shard_map/jit(remainder)/select_n | solution.py:17
  0.7 0.8 %compare_and_fusion = (pred[8,64]{1,0:T(8,128)(4,1)S(1)}, s32[8,64]{1,0:T(8,128)S(1)}, pred[8,64]{1,0:T(8,128)(4,1)S(1)}) fusion(s32[]{:T(128)S(6)} %axis_index.15, s32[8]{0:T(128)} %param.11, s32[8,64]{1,0:T(8,128)} %param.10), kind=kLoop, calls=%fused_computation.17 | loop fusion | flops 9216 | bytes 5156 | tf_op jit(solution)/shard_map/and | solution.py:24
  1.5 0.3 convert_reduce_fusion
  1.8 0.2 select_reduce_fusion.1
  2.1 0.6 reshape.116.send_idx
  2.7 0.2 select_reduce_fusion
  2.9 0.6 sub.14.slot_idx
  3.5 59.6 %shard_map.64 = bf16[1024,2048]{1,0:T(8,128)(2,1)} custom-call(s32[64]{0:T(128)} %reshape.116.send_idx, s32[64]{0:T(128)} %sub.14.slot_idx, s32[1,1024]{1,0:T(1,128)} %bitcast.7, bf16[32,16,1024]{2,1,0:T(8,128)(2,1)} %t2_hbm.1, bf16[1,64,16,2048]{3,2,1,0:T(8,128)(2,1)} %vp_hbm.1, bf16[1,64,16,2048]{3,2,1,0:T(8,128)(2,1)} %vm_hbm.1), custom_call_target="tpu_custom_call" | custom-call | flops 8589934592 | bytes 16777216 | tf_op jit(solution)/shard_map/pallas_call | solution.py:194
  63.2 4.8 %copy.8 = bf16[1024,2048]{1,0:T(8,128)(2,1)} copy(bf16[1024,2048]{1,0:T(8,128)(2,1)} %shard_map.64) | data formatting | bytes 8388608
  (7 shorter events, 0.0 us)

commit v2 on v1

--- a/solution.py
+++ b/solution.py
@@ -10,11 +10,16 @@
 MESH = pl.DeviceIdType.MESH
 
 
+def split_tile(tile, per_source):
+    if per_source & (per_source - 1) == 0:
+        return tile >> (per_source.bit_length() - 1), tile & (per_source - 1)
+    return tile // per_source, tile % per_source
+
+
 def route_plan(win_tile, win_count, per_source, capacity):
     owners, slots = win_tile.shape
     me = lax.axis_index("tiles")
-    sources = win_tile // per_source
-    offsets = win_tile % per_source
+    sources, offsets = split_tile(win_tile, per_source)
     positions = jnp.arange(slots)
     living = positions[None, :] < win_count[:, None]
     earlier = positions[None, None, :] < positions[None, :, None]
@@ -30,7 +35,7 @@
         & (mine[1][None, None, :] == ranks[None, :, None])
     )
     slot = jnp.sum(jnp.where(filled, positions + 1, 0), axis=2, dtype=jnp.int32) - 1
-    return send.reshape(-1), slot.reshape(-1)
+    return send, slot
 
 
 def across(me, n, d):
@@ -43,9 +48,9 @@
 
 def kernel(
     n, cap, order,
-    send_idx, slot_idx, partner, t2_hbm, vp_hbm, vm_hbm, out_hbm,
-    t2, vp, vm, pack, recv, mirror, onehot, vst, wt, acc, staged,
-    in_sem, send_sem, recv_sem, fwd_sem, mir_sem, out_sem,
+    send_idx, slot_idx, partner, t2, vp_hbm, vm_hbm, acc, wt, vst,
+    vp, vm, pack, recv, mirror, onehot,
+    in_sem, send_sem, recv_sem, fwd_sem, mir_sem,
 ):
     me = lax.axis_index("tiles")
     pair = lax.axis_index("pair")
@@ -55,10 +60,8 @@
     depth = cap * tw
     block = 512
 
-    t2_in = pltpu.make_async_copy(t2_hbm, t2, in_sem.at[0])
-    t2_in.start()
-    vp_in = pltpu.make_async_copy(vp_hbm.at[0], vp, in_sem.at[1])
-    vm_in = pltpu.make_async_copy(vm_hbm.at[0], vm, in_sem.at[2])
+    vp_in = pltpu.make_async_copy(vp_hbm.at[0], vp, in_sem.at[0])
+    vm_in = pltpu.make_async_copy(vm_hbm.at[0], vm, in_sem.at[1])
     vp_in.start()
     vm_in.start()
 
@@ -71,7 +74,6 @@
     lax.fori_loop(1, n, greet, 0)
     pl.semaphore_signal(barrier, inc=1, device_id={"pair": sibling}, device_id_type=MESH)
     pl.semaphore_wait(barrier, n)
-    t2_in.wait()
 
     def route(d):
         return pltpu.make_async_remote_copy(
@@ -88,7 +90,7 @@
     def fill(d):
         owner = across(me, n, d)
         for r in range(cap):
-            pack[d, r * tw : (r + 1) * tw] = t2[send_idx[owner * cap + r]]
+            pack[d, r * tw : (r + 1) * tw] = t2[send_idx[owner, r]]
 
     def dispatch(d):
         fill(d)
@@ -114,7 +116,7 @@
     def slabs(d):
         source = across(me, n, d)
         for r in range(cap):
-            slot = slot_idx[source * cap + r]
+            slot = slot_idx[source, r]
             at = jnp.maximum(slot, 0)
             keep = (slot >= 0).astype(jnp.float32).astype(jnp.bfloat16)
             vst[r * tw : (r + 1) * tw, :] = vp[at] * keep
@@ -161,15 +163,6 @@
         lax.fori_loop(1, n - 1, lambda j, c: (add(n - j), c)[1], 0)
         last = 1
     arrive(last)
-    writes = []
-    for i in range(cols // block):
-        at = i * block
-        staged[:, at : at + block] = (0.5 * (acc[:, at : at + block] + product(at))).astype(jnp.bfloat16)
-        write = pltpu.make_async_copy(
-            staged.at[:, at : at + block], out_hbm.at[:, at : at + block], out_sem.at[i]
-        )
-        write.start()
-        writes.append(write)
 
     def settle(d, carry):
         route(d).wait_send()
@@ -178,6 +171,19 @@
 
     lax.fori_loop(1, n, settle, 0)
     forward(0, pack).wait_send()
+
+
+def finish(acc, wt, vst, out_hbm, staged, out_sem):
+    cols = acc.shape[1]
+    block = 256
+    writes = []
+    for i in range(cols // block):
+        at = slice(i * block, (i + 1) * block)
+        total = acc[:, at] + jnp.dot(wt[...], vst[:, at], preferred_element_type=jnp.float32)
+        staged[:, at] = (0.5 * total).astype(jnp.bfloat16)
+        write = pltpu.make_async_copy(staged.at[:, at], out_hbm.at[:, at], out_sem.at[i])
+        write.start()
+        writes.append(write)
     for write in writes:
         write.wait()
 
@@ -190,38 +196,57 @@
     send, slot = route_plan(win_tile, win_count, per_source, cap)
     order = (7, 1, 6, 2, 5, 3, 4) if n == 8 else tuple(range(n - 1, 0, -1))
     depth = cap * tw
-    vmem, smem, hbm = pltpu.VMEM, pltpu.SMEM, pl.ANY
-    return pl.pallas_call(
+    vmem, smem, hbm = pltpu.VMEM, pltpu.SMEM, pltpu.HBM
+    partial, last_t, last_v = pl.pallas_call(
         functools.partial(kernel, n, cap, order),
-        out_shape=jax.ShapeDtypeStruct((rows, cols), jnp.bfloat16),
-        in_specs=[pl.BlockSpec(memory_space=m) for m in (smem, smem, vmem, hbm, hbm, hbm)],
-        out_specs=pl.BlockSpec(memory_space=hbm),
+        out_shape=(
+            jax.ShapeDtypeStruct((rows, cols), jnp.float32),
+            jax.ShapeDtypeStruct((rows, 2 * depth), jnp.bfloat16),
+            jax.ShapeDtypeStruct((2 * depth, cols), jnp.bfloat16),
+        ),
+        in_specs=[pl.BlockSpec(memory_space=m) for m in (smem, smem, vmem, vmem, hbm, hbm)],
+        out_specs=(pl.BlockSpec(memory_space=vmem),) * 3,
         scratch_shapes=[
-            pltpu.VMEM(t2.shape, jnp.bfloat16),
             pltpu.VMEM(v_plus.shape[1:], jnp.bfloat16),
             pltpu.VMEM(v_minus.shape[1:], jnp.bfloat16),
             pltpu.VMEM((n, depth, rows), jnp.bfloat16),
             pltpu.VMEM((n, depth, rows), jnp.bfloat16),
             pltpu.VMEM((n, depth, rows), jnp.bfloat16),
             pltpu.VMEM((rows, rows), jnp.bfloat16),
-            pltpu.VMEM((2 * depth, cols), jnp.bfloat16),
-            pltpu.VMEM((rows, 2 * depth), jnp.bfloat16),
-            pltpu.VMEM((rows, cols), jnp.float32),
-            pltpu.VMEM((rows, cols), jnp.bfloat16),
-            pltpu.SemaphoreType.DMA((3,)),
-            pltpu.SemaphoreType.DMA((n,)),
-            pltpu.SemaphoreType.DMA((n,)),
-            pltpu.SemaphoreType.DMA((n,)),
-            pltpu.SemaphoreType.DMA((n,)),
-            pltpu.SemaphoreType.DMA((cols // 512,)),
+            pltpu.SemaphoreType.DMA((2,)),
+            pltpu.SemaphoreType.DMA((n,)),
+            pltpu.SemaphoreType.DMA((n,)),
+            pltpu.SemaphoreType.DMA((n,)),
+            pltpu.SemaphoreType.DMA((n,)),
         ],
         compiler_params=pltpu.CompilerParams(
-            collective_id=0, has_side_effects=True, vmem_limit_bytes=56 * 2**20
+            collective_id=0, has_side_effects=True, vmem_limit_bytes=28 * 2**20
         ),
         cost_estimate=pl.CostEstimate(
             flops=4 * rows * cols * n * depth, bytes_accessed=16 * 2**20, transcendentals=0
         ),
-    )(send, slot, partner.reshape(1, rows), t2, v_plus, v_minus)
+    )(
+        send,
+        slot,
+        partner.reshape(1, rows),
+        t2,
+        pltpu.with_memory_space_constraint(v_plus, hbm),
+        pltpu.with_memory_space_constraint(v_minus, hbm),
+    )
+    return pl.pallas_call(
+        finish,
+        out_shape=jax.ShapeDtypeStruct((rows, cols), jnp.bfloat16),
+        in_specs=[pl.BlockSpec(memory_space=vmem)] * 3,
+        out_specs=pl.BlockSpec(memory_space=hbm),
+        scratch_shapes=[
+            pltpu.VMEM((rows, cols), jnp.bfloat16),
+            pltpu.SemaphoreType.DMA((cols // 256,)),
+        ],
+        compiler_params=pltpu.CompilerParams(vmem_limit_bytes=16 * 2**20),
+        cost_estimate=pl.CostEstimate(
+            flops=4 * rows * cols * depth, bytes_accessed=16 * 2**20, transcendentals=0
+        ),
+    )(partial, last_t, last_v)
 
 
 def solution(mesh):

time: 68.2 us -> 64.2 us (0.941)
  local copies, waits for them, and re-layouts: 6.01 us -> 1.93 us
    unnamed x1 -> x4, local copies, waits for them, and re-layouts: 4.79 us -> 1.91 us
    select_n x1 -> x0, other arithmetic: 0.69 us -> none  [route_plan(): offsets = win_tile % per_source]
    shift_right_arithmetic x0 -> x1, other arithmetic: none -> 0.69 us  [split_tile(): return (tile >> per_source.bit_length() - 1, tile & per_source - 1)]
    pallas_call x1 -> x2, Pallas kernels: 59.6 us -> 59.7 us  [the longest x1 57.1 us: body(): pl.pallas_call(functools.partial(kernel, n, cap, order), out_shape=(jax.S...]
where the time goes in v2:
time: 64.2 us; the launch traced here: 64 us
  Pallas kernels  59.7 us (93%)
  other arithmetic  2.24 us (3%)
  local copies, waits for them, and re-layouts  1.93 us (3%)
    pallas_call x1, Pallas kernels, body(): pl.pallas_call(functools.partial(kernel, n, cap, order), out_shape=(jax.S...  57.1 us
    pallas_call x1, Pallas kernels, body(): pl.pallas_call(finish, out_shape=jax.ShapeDtypeStruct((rows, cols), jnp.b...  2.59 us
    unnamed x4, local copies, waits for them, and re-layouts  1.91 us

profile of v2, /device:TPU:1, one launch (start us, length us, event | category | flops | bytes accessed | tf_op | source)
XLA Modules:
  0.0 64.0 jit_solution(4269401373205589190)
XLA Ops:
  0.0 0.8 %compare_and_fusion = (pred[8,64]{1,0:T(8,128)(4,1)S(1)}, pred[8,64]{1,0:T(8,128)(4,1)S(1)}) fusion(s32[]{:T(128)S(6)} %axis_index.15, s32[8,64]{1,0:T(8,128)} %param.10, s32[8]{0:T(128)} %param.11), kind=kLoop, calls=%fused_computation.10 | loop fusion | flops 2048 | bytes 3108 | tf_op jit(solution)/shard_map/and | solution.py:29
  0.8 0.7 %broadcast_shift-right-arithmetic_fusion = (s32[8,64]{1,0:T(8,128)S(1)}, s32[8,64]{1,0:T(8,128)S(1)}) fusion(s32[8,64]{1,0:T(8,128)} %param.10), kind=kLoop, calls=%fused_computation.13 | loop fusion | flops 1024 | bytes 6144 | tf_op jit(solution)/shard_map/shift_right_arithmetic | solution.py:15
  1.5 0.3 convert_reduce_fusion
  1.8 0.2 select_reduce_fusion.1.send_idx
  2.1 0.2 select_reduce_fusion
  2.3 0.0 copy-start
  2.3 1.2 %copy-done = bf16[32,16,1024]{2,1,0:T(8,128)(2,1)S(1)} copy-done((bf16[32,16,1024]{2,1,0:T(8,128)(2,1)S(1)}, bf16[32,16,1024]{2,1,0:T(8,128)(2,1)}, u32[]{:S(2)}) %copy-start) | copy-done | bytes 1048600
  3.5 0.0 copy-start.1
  3.5 0.7 %copy-done.1 = s32[1024]{0:T(1024)S(1)} copy-done((s32[1024]{0:T(1024)S(1)}, s32[1024]{0:T(1024)}, u32[]{:S(2)}) %copy-start.1) | copy-done | bytes 4120
  4.2 57.1 %shard_map.64 = (f32[1024,2048]{1,0:T(8,128)S(1)}, bf16[1024,256]{1,0:T(8,128)(2,1)S(1)}, bf16[256,2048]{1,0:T(8,128)(2,1)S(1)}) custom-call(s32[8,8]{1,0:T(8,128)S(1)} %select_reduce_fusion.1.send_idx, s32[8,8]{1,0:T(8,128)S(1)} %broadcast_add_fusion.slot_idx, s32[1,1024]{1,0:T(1,128)S(1)} %bitcast.7, bf16[32,16,1024]{2,1,0:T(8,128)(2,1)S(1)} %copy-done, ...), custom_call_target="tpu_custom_call" | custom-call | flops 8589934592 | bytes 16777216 | tf_op jit(solution)/shard_map/pallas_call | solution.py:200
  61.4 2.6 %shard_map.65 = bf16[1024,2048]{1,0:T(8,128)(2,1)} custom-call(f32[1024,2048]{1,0:T(8,128)S(1)} %get-tuple-element.8.acc, bf16[1024,256]{1,0:T(8,128)(2,1)S(1)} %get-tuple-element.9.wt, bf16[256,2048]{1,0:T(8,128)(2,1)S(1)} %get-tuple-element.10.vst), custom_call_target="tpu_custom_call" | custom-call | flops 1073741824 | bytes 16777216 | tf_op jit(solution)/shard_map/pallas_call | solution.py:236
  (7 shorter events, 0.1 us)
Async XLA Ops:
  2.3 1.2 %copy-start = (bf16[32,16,1024]{2,1,0:T(8,128)(2,1)S(1)}, bf16[32,16,1024]{2,1,0:T(8,128)(2,1)}, u32[]{:S(2)}) copy-start(bf16[32,16,1024]{2,1,0:T(8,128)(2,1)} %t2.1) | copy-start | bytes 3145732
  3.5 0.7 %copy-start.1 = (s32[1024]{0:T(1024)S(1)}, s32[1024]{0:T(1024)}, u32[]{:S(2)}) copy-start(s32[1024]{0:T(1024)} %param.9) | copy-start | bytes 12292

commit v3 on v2

v3 whole, which is shorter than its diff:
```python
import functools

import jax
import jax.numpy as jnp
from jax import lax
from jax.experimental import pallas as pl
from jax.experimental.pallas import tpu as pltpu
from jax.sharding import PartitionSpec as P

MESH = pl.DeviceIdType.MESH


def split_tile(tile, per_source):
    if per_source & (per_source - 1) == 0:
        return tile >> (per_source.bit_length() - 1), tile & (per_source - 1)
    return tile // per_source, tile % per_source


def route_plan(win_tile, win_count, per_source, capacity):
    owners, slots = win_tile.shape
    me = lax.axis_index("tiles")
    sources, offsets = split_tile(win_tile, per_source)
    positions = jnp.arange(slots)
    living = positions[None, :] < win_count[:, None]
    earlier = positions[None, None, :] < positions[None, :, None]
    same = (sources[:, :, None] == sources[:, None, :]) & living[:, None, :] & earlier
    ranked = jnp.sum(same, axis=2, dtype=jnp.int32)
    ranks = jnp.arange(capacity)
    taken = (living & (sources == me))[:, :, None] & (ranked[:, :, None] == ranks)
    send = jnp.sum(jnp.where(taken, offsets[:, :, None], 0), axis=1, dtype=jnp.int32)
    mine = [lax.dynamic_index_in_dim(x, me, 0, keepdims=False) for x in (sources, ranked, living)]
    filled = (
        mine[2][None, None, :]
        & (mine[0][None, None, :] == jnp.arange(owners)[:, None, None])
        & (mine[1][None, None, :] == ranks[None, :, None])
    )
    slot = jnp.sum(jnp.where(filled, positions + 1, 0), axis=2, dtype=jnp.int32) - 1
    return send, slot


def across(me, n, d):
    other, place = 0, 1
    while place < n:
        other = other + ((me // place) % 2 + (d // place) % 2) % 2 * place
        place *= 2
    return other


def kernel(
    n, cap, far, near,
    send_idx, slot_idx, partner_hbm, t2_hbm, vp_hbm, vm_hbm, acc, far_wt, far_vst,
    t2, partner, vp, vm, pack, recv, mirror, onehot, near_wt, near_vst,
    in_sem, send_sem, recv_sem, fwd_sem, mir_sem,
):
    me = lax.axis_index("tiles")
    pair = lax.axis_index("pair")
    sibling = pair + 1 - 2 * (pair % 2)
    tw, rows = t2.shape[1:]
    cols = vp.shape[2]
    halves, depth = pack.shape[1:3]
    per_half = cap // halves
    block = 512

    reads = [
        pltpu.make_async_copy(src, dst, in_sem.at[i])
        for i, (src, dst) in enumerate(
            [(t2_hbm, t2), (partner_hbm, partner), (vp_hbm.at[0], vp), (vm_hbm.at[0], vm)]
        )
    ]
    for read in reads:
        read.start()

    barrier = pltpu.get_barrier_semaphore()

    def greet(d, carry):
        pl.semaphore_signal(barrier, inc=1, device_id={"tiles": across(me, n, d)}, device_id_type=MESH)
        return carry

    lax.fori_loop(1, n, greet, 0)
    pl.semaphore_signal(barrier, inc=1, device_id={"pair": sibling}, device_id_type=MESH)
    reads[0].wait()

    def fill(d, h):
        owner = across(me, n, d)
        for r in range(per_half):
            pack[d, h, r * tw : (r + 1) * tw] = t2[send_idx[owner, h * per_half + r]]

    def route(d, h):
        return pltpu.make_async_remote_copy(
            src_ref=pack.at[d, h], dst_ref=recv.at[d, h],
            send_sem=send_sem.at[d, h], recv_sem=recv_sem.at[d, h],
            device_id={"tiles": across(me, n, d)}, device_id_type=MESH,
        )

    def forward(d, h, src):
        return pltpu.make_async_remote_copy(
            src_ref=src.at[d, h], dst_ref=mirror.at[d, h],
            send_sem=fwd_sem.at[d, h], recv_sem=mir_sem.at[d, h],
            device_id={"pair": sibling}, device_id_type=MESH,
        )

    far_pieces = [(d, h) for d in far for h in range(halves)]
    near_pieces = [(d, h) for d in near for h in range(halves)]
    ahead = 2
    if far:
        for piece in far_pieces[:ahead]:
            fill(*piece)
    pl.semaphore_wait(barrier, n)
    if far:
        for piece in far_pieces[:ahead]:
            route(*piece).start()
        for piece in near_pieces[:ahead]:
            fill(*piece)
            route(*piece).start()
        for piece in far_pieces[ahead:] + near_pieces[ahead:]:
            fill(*piece)
    else:
        def dispatch(j, carry):
            for h in range(halves):
                fill(n - j, h)
                route(n - j, h).start()
            return carry

        lax.fori_loop(1, n, dispatch, 0)
    for h in range(halves):
        fill(0, h)
        forward(0, h, pack).start()
    reads[1].wait()

    @pl.loop(0, rows // 128)
    def _(i):
        at = pl.multiple_of(i * 128, 128)
        row = lax.broadcasted_iota(jnp.int32, (128, rows), 0) + at
        onehot[pl.ds(at, 128), :] = (row == partner[...]).astype(jnp.float32).astype(jnp.bfloat16)

    reads[2].wait()
    reads[3].wait()

    def slabs(d, vst):
        source = across(me, n, d)
        for r in range(cap):
            slot = slot_idx[source, r]
            at = jnp.maximum(slot, 0)
            keep = (slot >= 0).astype(jnp.float32).astype(jnp.bfloat16)
            to = r // per_half * 2 * depth + r % per_half * tw
            vst[to : to + tw, :] = vp[at] * keep
            vst[to + depth : to + depth + tw, :] = vm[at] * keep

    def combine(d, h, src, wt):
        mir = jnp.dot(mirror[d, h], onehot[...], preferred_element_type=jnp.float32)
        own = src[d, h].astype(jnp.float32)
        both = jnp.concatenate([own + mir, own - mir], axis=0)
        wt[:, h * 2 * depth : (h + 1) * 2 * depth] = jnp.transpose(both).astype(jnp.bfloat16)

    def add(wt, vst, first=False):
        @pl.loop(0, cols // block)
        def _(i):
            at = pl.ds(pl.multiple_of(i * block, block), block)
            part = jnp.dot(wt[...], vst[:, at], preferred_element_type=jnp.float32)
            acc[:, at] = part if first else acc[:, at] + part

    def receive(d, h):
        route(d, h).wait_recv()
        forward(d, h, recv).start()

    def merge(d, h, wt):
        forward(d, h, recv).wait_recv()
        combine(d, h, recv, wt)

    slabs(0, near_vst)
    for h in range(halves):
        forward(0, h, pack).wait_recv()
        combine(0, h, pack, near_wt)
    add(near_wt, near_vst, True)

    if far:
        for k, (d, h) in enumerate(far_pieces):
            beside = near_pieces[k] if k < len(near_pieces) else None
            if h == 0:
                slabs(d, far_vst)
                if beside:
                    slabs(beside[0], near_vst)
            receive(d, h)
            if k + ahead < len(far_pieces):
                route(d, h).wait_send()
                route(*far_pieces[k + ahead]).start()
            if k + ahead < len(near_pieces):
                route(*near_pieces[k + ahead]).start()
            if beside:
                receive(*beside)
            merge(d, h, far_wt)
            if h == halves - 1 and k < len(far_pieces) - 1:
                add(far_wt, far_vst)
            if beside:
                merge(*beside, near_wt)
                if beside[1] == halves - 1:
                    add(near_wt, near_vst)
        for piece in far_pieces[-ahead:] + near_pieces:
            route(*piece).wait_send()
    else:
        def step(d):
            slabs(d, far_vst)
            for h in range(halves):
                receive(d, h)
                merge(d, h, far_wt)

        def whole_step(j, carry):
            step(n - j)
            add(far_wt, far_vst)
            return carry

        lax.fori_loop(1, n - 1, whole_step, 0)
        step(1)

    def settle(d, carry):
        for h in range(halves):
            if not far:
                route(d, h).wait_send()
            forward(d, h, recv).wait_send()
        return carry

    lax.fori_loop(1, n, settle, 0)
    for h in range(halves):
        forward(0, h, pack).wait_send()


def finish(acc, wt, vst, out_hbm, staged, out_sem):
    cols = acc.shape[1]
    block = 256
    writes = []
    for i in range(cols // block):
        at = slice(i * block, (i + 1) * block)
        total = acc[:, at] + jnp.dot(wt[...], vst[:, at], preferred_element_type=jnp.float32)
        staged[:, at] = (0.5 * total).astype(jnp.bfloat16)
        write = pltpu.make_async_copy(staged.at[:, at], out_hbm.at[:, at], out_sem.at[i])
        write.start()
        writes.append(write)
    for write in writes:
        write.wait()


def body(t2, v_plus, v_minus, partner, win_tile, win_count):
    per_source, tw, rows = t2.shape
    n = lax.axis_size("tiles")
    slots, cols = v_plus.shape[1], v_plus.shape[3]
    cap = max(2, (slots + n - 1) // n)
    send, slot = route_plan(win_tile, win_count, per_source, cap)
    halves = 2 if cap % 2 == 0 and cap * tw >= 128 else 1
    far, near = ((7, 6, 5, 4), (1, 2, 3)) if n == 8 else ((), ())
    depth = cap * tw
    pieces = (n, halves, depth // halves, rows)
    vmem, smem, hbm = pltpu.VMEM, pltpu.SMEM, pltpu.HBM
    partial, last_t, last_v = pl.pallas_call(
        functools.partial(kernel, n, cap, far, near),
        out_shape=(
            jax.ShapeDtypeStruct((rows, cols), jnp.float32),
            jax.ShapeDtypeStruct((rows, 2 * depth), jnp.bfloat16),
            jax.ShapeDtypeStruct((2 * depth, cols), jnp.bfloat16),
        ),
        in_specs=[pl.BlockSpec(memory_space=m) for m in (smem, smem, hbm, hbm, hbm, hbm)],
        out_specs=(pl.BlockSpec(memory_space=vmem),) * 3,
        scratch_shapes=[
            pltpu.VMEM(t2.shape, jnp.bfloat16),
            pltpu.VMEM((1, rows), jnp.int32),
            pltpu.VMEM(v_plus.shape[1:], jnp.bfloat16),
            pltpu.VMEM(v_minus.shape[1:], jnp.bfloat16),
            pltpu.VMEM(pieces, jnp.bfloat16),
            pltpu.VMEM(pieces, jnp.bfloat16),
            pltpu.VMEM(pieces, jnp.bfloat16),
            pltpu.VMEM((rows, rows), jnp.bfloat16),
            pltpu.VMEM((rows, 2 * depth), jnp.bfloat16),
            pltpu.VMEM((2 * depth, cols), jnp.bfloat16),
            pltpu.SemaphoreType.DMA((4,)),
            pltpu.SemaphoreType.DMA((n, halves)),
            pltpu.SemaphoreType.DMA((n, halves)),
            pltpu.SemaphoreType.DMA((n, halves)),
            pltpu.SemaphoreType.DMA((n, halves)),
        ],
        compiler_params=pltpu.CompilerParams(
            collective_id=0, has_side_effects=True, vmem_limit_bytes=30 * 2**20
        ),
        cost_estimate=pl.CostEstimate(
            flops=4 * rows * cols * n * depth, bytes_accessed=16 * 2**20, transcendentals=0
        ),
    )(
        send,
        slot,
        pltpu.with_memory_space_constraint(partner.reshape(1, rows), hbm),
        pltpu.with_memory_space_constraint(t2, hbm),
        pltpu.with_memory_space_constraint(v_plus, hbm),
        pltpu.with_memory_space_constraint(v_minus, hbm),
    )
    return pl.pallas_call(
        finish,
        out_shape=jax.ShapeDtypeStruct((rows, cols), jnp.bfloat16),
        in_specs=[pl.BlockSpec(memory_space=vmem)] * 3,
        out_specs=pl.BlockSpec(memory_space=hbm),
        scratch_shapes=[
            pltpu.VMEM((rows, cols), jnp.bfloat16),
            pltpu.SemaphoreType.DMA((cols // 256,)),
        ],
        compiler_params=pltpu.CompilerParams(vmem_limit_bytes=16 * 2**20),
        cost_estimate=pl.CostEstimate(
            flops=4 * rows * cols * depth, bytes_accessed=16 * 2**20, transcendentals=0
        ),
    )(partial, last_t, last_v)


def solution(mesh):
    placed = (
        P("tiles", None, "pair"),
        P("tiles", None, None, None),
        P("tiles", None, None, None),
        P("pair"),
        P(),
        P(),
    )
    return jax.shard_map(
        body, mesh=mesh, in_specs=placed, out_specs=P("pair", "tiles"), check_vma=False
    )
```

time: 64.2 us -> 60.3 us (0.939)
  Pallas kernels: 59.7 us -> 57.6 us
  local copies, waits for them, and re-layouts: 1.93 us -> 0.02 us
    pallas_call x1, Pallas kernels: 57.1 us -> 55 us  [body(): pl.pallas_call(functools.partial(kernel, n, cap, far, near), out_shape=(j...]
    unnamed x4 -> x0, local copies, waits for them, and re-layouts: 1.91 us -> none
where the time goes in v3:
time: 60.3 us; the launch traced here: 59.9 us
  Pallas kernels  57.6 us (96%)
  other arithmetic  2.24 us (4%)
    pallas_call x1, Pallas kernels, body(): pl.pallas_call(functools.partial(kernel, n, cap, far, near), out_shape=(j...  55 us
    pallas_call x1, Pallas kernels, body(): pl.pallas_call(finish, out_shape=jax.ShapeDtypeStruct((rows, cols), jnp.b...  2.6 us

profile of v3, /device:TPU:1, one launch (start us, length us, event | category | flops | bytes accessed | tf_op | source)
XLA Modules:
  0.0 59.9 jit_solution(4282698143943883314)
XLA Ops:
  0.0 0.8 %compare_and_fusion = (pred[8,64]{1,0:T(8,128)(4,1)S(1)}, pred[8,64]{1,0:T(8,128)(4,1)S(1)}) fusion(s32[]{:T(128)S(6)} %axis_index.15, s32[8,64]{1,0:T(8,128)} %param.10, s32[8]{0:T(128)} %param.11), kind=kLoop, calls=%fused_computation.10 | loop fusion | flops 2048 | bytes 3108 | tf_op jit(solution)/shard_map/and | solution.py:29
  0.8 0.7 %broadcast_shift-right-arithmetic_fusion = (s32[8,64]{1,0:T(8,128)S(1)}, s32[8,64]{1,0:T(8,128)S(1)}) fusion(s32[8,64]{1,0:T(8,128)} %param.10), kind=kLoop, calls=%fused_computation.13 | loop fusion | flops 1024 | bytes 6144 | tf_op jit(solution)/shard_map/shift_right_arithmetic | solution.py:15
  1.5 0.3 convert_reduce_fusion
  1.8 0.2 select_reduce_fusion.1.send_idx
  2.1 0.2 select_reduce_fusion
  2.3 55.0 %shard_map.64 = (f32[1024,2048]{1,0:T(8,128)S(1)}, bf16[1024,256]{1,0:T(8,128)(2,1)S(1)}, bf16[256,2048]{1,0:T(8,128)(2,1)S(1)}) custom-call(s32[8,8]{1,0:T(8,128)S(1)} %select_reduce_fusion.1.send_idx, s32[8,8]{1,0:T(8,128)S(1)} %broadcast_add_fusion.slot_idx, s32[1,1024]{1,0:T(1,128)} %bitcast.7, bf16[32,16,1024]{2,1,0:T(8,128)(2,1)} %t2_hbm.1, ...), custom_call_target="tpu_custom_call" | custom-call | flops 8589934592 | bytes 16777216 | tf_op jit(solution)/shard_map/pallas_call | solution.py:253
  57.3 2.6 %shard_map.65 = bf16[1024,2048]{1,0:T(8,128)(2,1)} custom-call(f32[1024,2048]{1,0:T(8,128)S(1)} %get-tuple-element.8.acc, bf16[1024,256]{1,0:T(8,128)(2,1)S(1)} %get-tuple-element.9.wt, bf16[256,2048]{1,0:T(8,128)(2,1)S(1)} %get-tuple-element.10.vst), custom_call_target="tpu_custom_call" | custom-call | flops 1073741824 | bytes 16777216 | tf_op jit(solution)/shard_map/pallas_call | solution.py:293
  (7 shorter events, 0.1 us)

commit v4 on v3

--- a/solution.py
+++ b/solution.py
@@ -16,26 +16,28 @@
     return tile // per_source, tile % per_source
 
 
-def route_plan(win_tile, win_count, per_source, capacity):
-    owners, slots = win_tile.shape
-    me = lax.axis_index("tiles")
-    sources, offsets = split_tile(win_tile, per_source)
-    positions = jnp.arange(slots)
-    living = positions[None, :] < win_count[:, None]
-    earlier = positions[None, None, :] < positions[None, :, None]
-    same = (sources[:, :, None] == sources[:, None, :]) & living[:, None, :] & earlier
-    ranked = jnp.sum(same, axis=2, dtype=jnp.int32)
-    ranks = jnp.arange(capacity)
-    taken = (living & (sources == me))[:, :, None] & (ranked[:, :, None] == ranks)
-    send = jnp.sum(jnp.where(taken, offsets[:, :, None], 0), axis=1, dtype=jnp.int32)
-    mine = [lax.dynamic_index_in_dim(x, me, 0, keepdims=False) for x in (sources, ranked, living)]
-    filled = (
-        mine[2][None, None, :]
-        & (mine[0][None, None, :] == jnp.arange(owners)[:, None, None])
-        & (mine[1][None, None, :] == ranks[None, :, None])
-    )
-    slot = jnp.sum(jnp.where(filled, positions + 1, 0), axis=2, dtype=jnp.int32) - 1
-    return send, slot
+def route_plan(tiles, row, counts, me, per_source, capacity):
+    n, slots = tiles.shape
+    none, shift = 2**30, 16
+    index = lax.broadcasted_iota(jnp.int32, (n, slots), 0)
+    slot = lax.broadcasted_iota(jnp.int32, (n, slots), 1)
+    count = jnp.zeros((n, slots), jnp.int32)
+    for o in range(n):
+        count = jnp.where(index == o, counts[o], count)
+    source, offset = split_tile(tiles, per_source)
+    sends = jnp.where((source == me) & (slot < count), (slot << shift) + offset, none)
+    source, _ = split_tile(row, per_source)
+    fills = jnp.where((source == index) & (slot < counts[me]), slot << shift, none)
+    keys = jnp.concatenate([sends, fills], axis=0)
+    lane = lax.broadcasted_iota(jnp.int32, (2 * n, 128), 1)
+    plan = jnp.full((2 * n, 128), none, jnp.int32)
+    for r in range(capacity):
+        first = jnp.min(keys, axis=1, keepdims=True)
+        plan = jnp.where(lane == r, first, plan)
+        keys = jnp.where(keys == first, none, keys)
+    sending = lax.broadcasted_iota(jnp.int32, (2 * n, 128), 0) < n
+    found = jnp.where(sending, plan & (2**shift - 1), plan >> shift)
+    return jnp.where(plan == none, jnp.where(sending, 0, -1), found)
 
 
 def across(me, n, d):
@@ -48,8 +50,8 @@
 
 def kernel(
     n, cap, far, near,
-    send_idx, slot_idx, partner_hbm, t2_hbm, vp_hbm, vm_hbm, acc, far_wt, far_vst,
-    t2, partner, vp, vm, pack, recv, mirror, onehot, near_wt, near_vst,
+    counts_hbm, win_hbm, partner_hbm, t2_hbm, vp_hbm, vm_hbm, acc, far_wt, far_vst,
+    counts, win, plan, plan_idx, t2, partner, vp, vm, pack, recv, mirror, onehot, near_wt, near_vst,
     in_sem, send_sem, recv_sem, fwd_sem, mir_sem,
 ):
     me = lax.axis_index("tiles")
@@ -64,7 +66,14 @@
     reads = [
         pltpu.make_async_copy(src, dst, in_sem.at[i])
         for i, (src, dst) in enumerate(
-            [(t2_hbm, t2), (partner_hbm, partner), (vp_hbm.at[0], vp), (vm_hbm.at[0], vm)]
+            [
+                (win_hbm, win),
+                (t2_hbm, t2),
+                (partner_hbm, partner),
+                (vp_hbm.at[0], vp),
+                (vm_hbm.at[0], vm),
+                (counts_hbm, counts),
+            ]
         )
     ]
     for read in reads:
@@ -79,11 +88,17 @@
     lax.fori_loop(1, n, greet, 0)
     pl.semaphore_signal(barrier, inc=1, device_id={"pair": sibling}, device_id_type=MESH)
     reads[0].wait()
+    reads[5].wait()
+    plan[...] = route_plan(win[...], win[pl.ds(me, 1), :], counts, me, t2.shape[0], cap)
+    to_smem = pltpu.make_async_copy(plan, plan_idx, in_sem.at[6])
+    to_smem.start()
+    to_smem.wait()
+    reads[1].wait()
 
     def fill(d, h):
         owner = across(me, n, d)
         for r in range(per_half):
-            pack[d, h, r * tw : (r + 1) * tw] = t2[send_idx[owner, h * per_half + r]]
+            pack[d, h, r * tw : (r + 1) * tw] = t2[plan_idx[owner, h * per_half + r]]
 
     def route(d, h):
         return pltpu.make_async_remote_copy(
@@ -125,7 +140,7 @@
     for h in range(halves):
         fill(0, h)
         forward(0, h, pack).start()
-    reads[1].wait()
+    reads[2].wait()
 
     @pl.loop(0, rows // 128)
     def _(i):
@@ -133,13 +148,13 @@
         row = lax.broadcasted_iota(jnp.int32, (128, rows), 0) + at
         onehot[pl.ds(at, 128), :] = (row == partner[...]).astype(jnp.float32).astype(jnp.bfloat16)
 
-    reads[2].wait()
     reads[3].wait()
+    reads[4].wait()
 
     def slabs(d, vst):
         source = across(me, n, d)
         for r in range(cap):
-            slot = slot_idx[source, r]
+            slot = plan_idx[n + source, r]
             at = jnp.maximum(slot, 0)
             keep = (slot >= 0).astype(jnp.float32).astype(jnp.bfloat16)
             to = r // per_half * 2 * depth + r % per_half * tw
@@ -225,14 +240,14 @@
 
 
 def finish(acc, wt, vst, out_hbm, staged, out_sem):
-    cols = acc.shape[1]
+    rows = acc.shape[0]
     block = 256
     writes = []
-    for i in range(cols // block):
+    for i in range(rows // block):
         at = slice(i * block, (i + 1) * block)
-        total = acc[:, at] + jnp.dot(wt[...], vst[:, at], preferred_element_type=jnp.float32)
-        staged[:, at] = (0.5 * total).astype(jnp.bfloat16)
-        write = pltpu.make_async_copy(staged.at[:, at], out_hbm.at[:, at], out_sem.at[i])
+        total = acc[at, :] + jnp.dot(wt[at, :], vst[...], preferred_element_type=jnp.float32)
+        staged[at, :] = (0.5 * total).astype(jnp.bfloat16)
+        write = pltpu.make_async_copy(staged.at[at, :], out_hbm.at[at, :], out_sem.at[i])
         write.start()
         writes.append(write)
     for write in writes:
@@ -240,16 +255,15 @@
 
 
 def body(t2, v_plus, v_minus, partner, win_tile, win_count):
-    per_source, tw, rows = t2.shape
+    tw, rows = t2.shape[1:]
     n = lax.axis_size("tiles")
     slots, cols = v_plus.shape[1], v_plus.shape[3]
     cap = max(2, (slots + n - 1) // n)
-    send, slot = route_plan(win_tile, win_count, per_source, cap)
     halves = 2 if cap % 2 == 0 and cap * tw >= 128 else 1
     far, near = ((7, 6, 5, 4), (1, 2, 3)) if n == 8 else ((), ())
     depth = cap * tw
     pieces = (n, halves, depth // halves, rows)
-    vmem, smem, hbm = pltpu.VMEM, pltpu.SMEM, pltpu.HBM
+    vmem, hbm = pltpu.VMEM, pltpu.HBM
     partial, last_t, last_v = pl.pallas_call(
         functools.partial(kernel, n, cap, far, near),
         out_shape=(
@@ -257,9 +271,13 @@
             jax.ShapeDtypeStruct((rows, 2 * depth), jnp.bfloat16),
             jax.ShapeDtypeStruct((2 * depth, cols), jnp.bfloat16),
         ),
-        in_specs=[pl.BlockSpec(memory_space=m) for m in (smem, smem, hbm, hbm, hbm, hbm)],
+        in_specs=[pl.BlockSpec(memory_space=hbm)] * 6,
         out_specs=(pl.BlockSpec(memory_space=vmem),) * 3,
         scratch_shapes=[
+            pltpu.SMEM(win_count.shape, jnp.int32),
+            pltpu.VMEM(win_tile.shape, jnp.int32),
+            pltpu.VMEM((2 * n, 128), jnp.int32),
+            pltpu.SMEM((2 * n, 128), jnp.int32),
             pltpu.VMEM(t2.shape, jnp.bfloat16),
             pltpu.VMEM((1, rows), jnp.int32),
             pltpu.VMEM(v_plus.shape[1:], jnp.bfloat16),
@@ -270,7 +288,7 @@
             pltpu.VMEM((rows, rows), jnp.bfloat16),
             pltpu.VMEM((rows, 2 * depth), jnp.bfloat16),
             pltpu.VMEM((2 * depth, cols), jnp.bfloat16),
-            pltpu.SemaphoreType.DMA((4,)),
+            pltpu.SemaphoreType.DMA((7,)),
             pltpu.SemaphoreType.DMA((n, halves)),
             pltpu.SemaphoreType.DMA((n, halves)),
             pltpu.SemaphoreType.DMA((n, halves)),
@@ -283,8 +301,8 @@
             flops=4 * rows * cols * n * depth, bytes_accessed=16 * 2**20, transcendentals=0
         ),
     )(
-        send,
-        slot,
+        pltpu.with_memory_space_constraint(win_count, hbm),
+        pltpu.with_memory_space_constraint(win_tile, hbm),
         pltpu.with_memory_space_constraint(partner.reshape(1, rows), hbm),
         pltpu.with_memory_space_constraint(t2, hbm),
         pltpu.with_memory_space_constraint(v_plus, hbm),
@@ -297,7 +315,7 @@
         out_specs=pl.BlockSpec(memory_space=hbm),
         scratch_shapes=[
             pltpu.VMEM((rows, cols), jnp.bfloat16),
-            pltpu.SemaphoreType.DMA((cols // 256,)),
+            pltpu.SemaphoreType.DMA((rows // 256,)),
         ],
         compiler_params=pltpu.CompilerParams(vmem_limit_bytes=16 * 2**20),
         cost_estimate=pl.CostEstimate(

time: 60.3 us -> 57.5 us (0.954)
  other arithmetic: 2.24 us -> 0 us
    and x2 -> x0, other arithmetic: 0.77 us -> none  [the longest x1 0.76 us: route_plan(): living & (sources == me)]
    reduce_sum x3 -> x0, other arithmetic: 0.75 us -> none  [the longest x1 0.32 us: route_plan(): ranked = jnp.sum(same, axis=2, dtype=jnp.int32)]
    shift_right_arithmetic x1 -> x0, other arithmetic: 0.69 us -> none  [split_tile(): return (tile >> per_source.bit_length() - 1, tile & per_source - 1)]
where the time goes in v4:
time: 57.5 us; the launch traced here: 57.3 us
  Pallas kernels  57.3 us (100%)
    pallas_call x1, Pallas kernels, body(): pl.pallas_call(functools.partial(kernel, n, cap, far, near), out_shape=(j...  54.8 us
    pallas_call x1, Pallas kernels, body(): pl.pallas_call(finish, out_shape=jax.ShapeDtypeStruct((rows, cols), jnp.b...  2.48 us

profile of v4, /device:TPU:1, one launch (start us, length us, event | category | flops | bytes accessed | tf_op | source)
XLA Modules:
  0.0 57.3 jit_solution(10632260752827176919)
XLA Ops:
  0.0 54.8 %shard_map.64 = (f32[1024,2048]{1,0:T(8,128)S(1)}, bf16[1024,256]{1,0:T(8,128)(2,1)S(1)}, bf16[256,2048]{1,0:T(8,128)(2,1)S(1)}) custom-call(s32[8]{0:T(128)} %counts_hbm.1, s32[8,64]{1,0:T(8,128)} %win_hbm.1, s32[1,1024]{1,0:T(1,128)} %bitcast.1, bf16[32,16,1024]{2,1,0:T(8,128)(2,1)} %t2_hbm.1, bf16[1,64,16,2048]{3,2,1,0:T(8,128)(2,1)} %vp_hbm.1, ...), custom_call_target="tpu_custom_call" | custom-call | flops 8589934592 | bytes 16777216 | tf_op jit(solution)/shard_map/pallas_call | solution.py:267
  54.9 2.5 %shard_map.65 = bf16[1024,2048]{1,0:T(8,128)(2,1)} custom-call(f32[1024,2048]{1,0:T(8,128)S(1)} %get-tuple-element.8.acc, bf16[1024,256]{1,0:T(8,128)(2,1)S(1)} %get-tuple-element.9.wt, bf16[256,2048]{1,0:T(8,128)(2,1)S(1)} %get-tuple-element.10.vst), custom_call_target="tpu_custom_call" | custom-call | flops 1073741824 | bytes 16777216 | tf_op jit(solution)/shard_map/pallas_call | solution.py:311

commit v5 on v4

--- a/solution.py
+++ b/solution.py
@@ -116,7 +116,7 @@
 
     far_pieces = [(d, h) for d in far for h in range(halves)]
     near_pieces = [(d, h) for d in near for h in range(halves)]
-    ahead = 2
+    ahead, beside_ahead = 3, 2
     if far:
         for piece in far_pieces[:ahead]:
             fill(*piece)
@@ -124,10 +124,10 @@
     if far:
         for piece in far_pieces[:ahead]:
             route(*piece).start()
-        for piece in near_pieces[:ahead]:
+        for piece in near_pieces[:beside_ahead]:
             fill(*piece)
             route(*piece).start()
-        for piece in far_pieces[ahead:] + near_pieces[ahead:]:
+        for piece in far_pieces[ahead:] + near_pieces[beside_ahead:]:
             fill(*piece)
     else:
         def dispatch(j, carry):
@@ -195,12 +195,12 @@
                 slabs(d, far_vst)
                 if beside:
                     slabs(beside[0], near_vst)
-            receive(d, h)
             if k + ahead < len(far_pieces):
                 route(d, h).wait_send()
                 route(*far_pieces[k + ahead]).start()
-            if k + ahead < len(near_pieces):
-                route(*near_pieces[k + ahead]).start()
+            if k + beside_ahead < len(near_pieces):
+                route(*near_pieces[k + beside_ahead]).start()
+            receive(d, h)
             if beside:
                 receive(*beside)
             merge(d, h, far_wt)

time: 57.5 us -> 63.3 us (1.10)
  the two profiles are of different devices: /device:TPU:1 before, /device:TPU:3 now
where the time goes in v5:
time: 63.3 us; the launch traced here: 63.2 us
  Pallas kernels  63.2 us (100%)
    pallas_call x1, Pallas kernels, body(): pl.pallas_call(functools.partial(kernel, n, cap, far, near), out_shape=(j...  60.7 us
    pallas_call x1, Pallas kernels, body(): pl.pallas_call(finish, out_shape=jax.ShapeDtypeStruct((rows, cols), jnp.b...  2.48 us

profile of v5, /device:TPU:3, one launch (start us, length us, event | category | flops | bytes accessed | tf_op | source)
XLA Modules:
  0.0 63.2 jit_solution(14870071045170712872)
XLA Ops:
  0.0 60.7 %shard_map.64 = (f32[1024,2048]{1,0:T(8,128)S(1)}, bf16[1024,256]{1,0:T(8,128)(2,1)S(1)}, bf16[256,2048]{1,0:T(8,128)(2,1)S(1)}) custom-call(s32[8]{0:T(128)} %counts_hbm.1, s32[8,64]{1,0:T(8,128)} %win_hbm.1, s32[1,1024]{1,0:T(1,128)} %bitcast.1, bf16[32,16,1024]{2,1,0:T(8,128)(2,1)} %t2_hbm.1, bf16[1,64,16,2048]{3,2,1,0:T(8,128)(2,1)} %vp_hbm.1, ...), custom_call_target="tpu_custom_call" | custom-call | flops 8589934592 | bytes 16777216 | tf_op jit(solution)/shard_map/pallas_call | solution.py:267
  60.7 2.5 %shard_map.65 = bf16[1024,2048]{1,0:T(8,128)(2,1)} custom-call(f32[1024,2048]{1,0:T(8,128)S(1)} %get-tuple-element.8.acc, bf16[1024,256]{1,0:T(8,128)(2,1)S(1)} %get-tuple-element.9.wt, bf16[256,2048]{1,0:T(8,128)(2,1)S(1)} %get-tuple-element.10.vst), custom_call_target="tpu_custom_call" | custom-call | flops 1073741824 | bytes 16777216 | tf_op jit(solution)/shard_map/pallas_call | solution.py:311

commit v6 on v4

--- a/solution.py
+++ b/solution.py
@@ -116,7 +116,7 @@
 
     far_pieces = [(d, h) for d in far for h in range(halves)]
     near_pieces = [(d, h) for d in near for h in range(halves)]
-    ahead = 2
+    ahead = 1
     if far:
         for piece in far_pieces[:ahead]:
             fill(*piece)

time: 57.5 us -> 66.9 us (1.16)
  the two profiles are of different devices: /device:TPU:1 before, /device:TPU:5 now
where the time goes in v6:
time: 66.9 us; the launch traced here: 66.7 us
  Pallas kernels  66.7 us (100%)
    pallas_call x1, Pallas kernels, body(): pl.pallas_call(functools.partial(kernel, n, cap, far, near), out_shape=(j...  64.2 us
    pallas_call x1, Pallas kernels, body(): pl.pallas_call(finish, out_shape=jax.ShapeDtypeStruct((rows, cols), jnp.b...  2.48 us

profile of v6, /device:TPU:5, one launch (start us, length us, event | category | flops | bytes accessed | tf_op | source)
XLA Modules:
  0.0 66.7 jit_solution(1252238444575086329)
XLA Ops:
  0.0 64.2 %shard_map.64 = (f32[1024,2048]{1,0:T(8,128)S(1)}, bf16[1024,256]{1,0:T(8,128)(2,1)S(1)}, bf16[256,2048]{1,0:T(8,128)(2,1)S(1)}) custom-call(s32[8]{0:T(128)} %counts_hbm.1, s32[8,64]{1,0:T(8,128)} %win_hbm.1, s32[1,1024]{1,0:T(1,128)} %bitcast.1, bf16[32,16,1024]{2,1,0:T(8,128)(2,1)} %t2_hbm.1, bf16[1,64,16,2048]{3,2,1,0:T(8,128)(2,1)} %vp_hbm.1, ...), custom_call_target="tpu_custom_call" | custom-call | flops 8589934592 | bytes 16777216 | tf_op jit(solution)/shard_map/pallas_call | solution.py:267
  64.2 2.5 %shard_map.65 = bf16[1024,2048]{1,0:T(8,128)(2,1)} custom-call(f32[1024,2048]{1,0:T(8,128)S(1)} %get-tuple-element.8.acc, bf16[1024,256]{1,0:T(8,128)(2,1)S(1)} %get-tuple-element.9.wt, bf16[256,2048]{1,0:T(8,128)(2,1)S(1)} %get-tuple-element.10.vst), custom_call_target="tpu_custom_call" | custom-call | flops 1073741824 | bytes 16777216 | tf_op jit(solution)/shard_map/pallas_call | solution.py:311

commit v7 on v5

--- a/solution.py
+++ b/solution.py
@@ -195,12 +195,12 @@
                 slabs(d, far_vst)
                 if beside:
                     slabs(beside[0], near_vst)
+            receive(d, h)
             if k + ahead < len(far_pieces):
                 route(d, h).wait_send()
                 route(*far_pieces[k + ahead]).start()
             if k + beside_ahead < len(near_pieces):
                 route(*near_pieces[k + beside_ahead]).start()
-            receive(d, h)
             if beside:
                 receive(*beside)
             merge(d, h, far_wt)

time: 63.3 us -> 65.3 us (1.032)
  the two profiles are of different devices: /device:TPU:3 before, /device:TPU:1 now
where the time goes in v7:
time: 65.3 us; the launch traced here: 64.7 us
  Pallas kernels  64.7 us (99%)
    pallas_call x1, Pallas kernels, body(): pl.pallas_call(functools.partial(kernel, n, cap, far, near), out_shape=(j...  62.2 us
    pallas_call x1, Pallas kernels, body(): pl.pallas_call(finish, out_shape=jax.ShapeDtypeStruct((rows, cols), jnp.b...  2.48 us

profile of v7, /device:TPU:1, one launch (start us, length us, event | category | flops | bytes accessed | tf_op | source)
XLA Modules:
  0.0 64.7 jit_solution(16361423946262292072)
XLA Ops:
  0.0 62.2 %shard_map.64 = (f32[1024,2048]{1,0:T(8,128)S(1)}, bf16[1024,256]{1,0:T(8,128)(2,1)S(1)}, bf16[256,2048]{1,0:T(8,128)(2,1)S(1)}) custom-call(s32[8]{0:T(128)} %counts_hbm.1, s32[8,64]{1,0:T(8,128)} %win_hbm.1, s32[1,1024]{1,0:T(1,128)} %bitcast.1, bf16[32,16,1024]{2,1,0:T(8,128)(2,1)} %t2_hbm.1, bf16[1,64,16,2048]{3,2,1,0:T(8,128)(2,1)} %vp_hbm.1, ...), custom_call_target="tpu_custom_call" | custom-call | flops 8589934592 | bytes 16777216 | tf_op jit(solution)/shard_map/pallas_call | solution.py:267
  62.2 2.5 %shard_map.65 = bf16[1024,2048]{1,0:T(8,128)(2,1)} custom-call(f32[1024,2048]{1,0:T(8,128)S(1)} %get-tuple-element.8.acc, bf16[1024,256]{1,0:T(8,128)(2,1)S(1)} %get-tuple-element.9.wt, bf16[256,2048]{1,0:T(8,128)(2,1)S(1)} %get-tuple-element.10.vst), custom_call_target="tpu_custom_call" | custom-call | flops 1073741824 | bytes 16777216 | tf_op jit(solution)/shard_map/pallas_call | solution.py:311
